TPU v7x, 32 devices: a whole 2x2x4 slice. The times are simulated.
32 devices in a mesh: dp: 2 (over x), ctx: 16 (over z, y, core).
Axes of the slice: x: 2, y: 2, z: 4, core: 2. Of those that a mesh axis runs over, the one named last changes fastest.
Arguments:
- inputs: bfloat16 [4, 2048, 960], P('dp', 'ctx'), may hold values from -16 to 16
- query_weight: bfloat16 [960, 960], P('ctx', 'dp'), may hold values from -0.1613743 to 0.1613743
- key_weight: bfloat16 [960, 320], P('ctx', 'dp'), may hold values from -0.1613743 to 0.1613743
- value_matrix: bfloat16 [960, 320], P('ctx', 'dp'), may hold values from -0.1875 to 0.1875
- out_weight: bfloat16 [960, 960], P('dp', 'ctx'), may hold values from -1.5 to 1.5
- gate_weight: bfloat16 [960, 2560], P('ctx', 'dp'), may hold values from -0.1875 to 0.1875
- up_weight: bfloat16 [960, 2560], P('ctx', 'dp'), may hold values from -0.1875 to 0.1875
- down_weight: bfloat16 [2560, 960], P('dp', 'ctx'), may hold values from -0.125 to 0.125
- norm_gains: bfloat16 [2, 960], P('dp', 'ctx'), may hold values from 0.5 to 1.5
- cotangent: bfloat16 [4, 2048, 960], P('dp', 'ctx'), may hold values from -6 to 6
Outputs:
- layer_out: bfloat16 [4, 2048, 960], P('dp', 'ctx')
- input_grad: float32 [4, 2048, 960], P('dp', 'ctx')
- query_grad: float32 [960, 960], P('ctx', 'dp')
- key_grad: float32 [960, 320], P('ctx', 'dp')
- value_grad: float32 [960, 320], P('ctx', 'dp')
- out_grad: float32 [960, 960], P('dp', 'ctx')
- gate_grad: float32 [960, 2560], P('ctx', 'dp')
- up_grad: float32 [960, 2560], P('ctx', 'dp')
- down_grad: float32 [2560, 960], P('dp', 'ctx')
- gains_grad: float32 [2, 960], P('dp', 'ctx')
All inputs are finite; a program needn't handle non-finite values.
Results may differ from a plain program's by a relative error of at most 0.02.
Values may be sent and summed in bfloat16 or wider, within the bound.
No kernel may reach another device: no remote copies, remote signals or barrier semaphores. Data moves between devices by JAX's collectives and lax.ppermute only.
A program may use at most 256 MiB of HBM per device.

v0:
```python
import math

import jax
import jax.numpy as jnp
from jax import lax
from jax.sharding import PartitionSpec as P

HEAD_WIDTH = 64


EPSILON = 1e-05
MASKED_SCORE = -1e30


def block_size(rows):
    current_size = 512
    while rows % current_size:
        current_size //= 2
    return current_size


def rope_tables(positions, half_width):
    spectrum = jnp.exp(
        jnp.arange(half_width, dtype=jnp.float32) * (-math.log(100000.0) / half_width)
    )
    angles = positions.astype(jnp.float32)[:, None] * spectrum[None, :]
    return (jnp.cos(angles), jnp.sin(angles))


def apply_rotation(vectors, cosine_table, sine_table):
    half_width = vectors.shape[-1] // 2
    low_half = vectors[..., :half_width]
    high_half = vectors[..., half_width:]
    cos_rows = cosine_table[:, None, :]
    sin_rows = sine_table[:, None, :]
    return jnp.concatenate(
        [low_half * cos_rows - high_half * sin_rows, high_half * cos_rows + low_half * sin_rows],
        axis=-1,
    )


def unrotate(vectors, cosine_table, sine_table):
    half_width = vectors.shape[-1] // 2
    low_half = vectors[..., :half_width]
    high_half = vectors[..., half_width:]
    cos_rows = cosine_table[:, None, :]
    sin_rows = sine_table[:, None, :]
    return jnp.concatenate(
        [low_half * cos_rows + high_half * sin_rows, high_half * cos_rows - low_half * sin_rows],
        axis=-1,
    )


def attend_block(state_now, query_rows, key_rows, value_row_list, query_pos, key_pos):
    run_max, run_sum, weighted = state_now
    scores = (
        jnp.einsum("srkgd,stkd->srkgt", query_rows, key_rows, preferred_element_type=jnp.float32)
        * 0.125
    )
    allowed = (query_pos[:, None] >= key_pos[None, :])[None, :, None, None, :]
    scores = jnp.where(allowed, scores, MASKED_SCORE)
    new_max = jnp.maximum(run_max, jnp.max(scores, axis=-1))
    shifted = jnp.where(allowed, jnp.exp(scores - new_max[..., None]), 0.0)
    rescale = jnp.exp(run_max - new_max)
    run_sum = run_sum * rescale + jnp.sum(shifted, axis=-1)
    weighted = weighted * rescale[..., None] + jnp.einsum(
        "srkgt,stkd->srkgd",
        shifted.astype(jnp.bfloat16),
        value_row_list,
        preferred_element_type=jnp.float32,
    )
    return (new_max, run_sum, weighted)


def grad_block(
    query_rows, back_attend, log_total, row_dot, key_rows, value_row_list, query_pos, key_pos
):
    scores = (
        jnp.einsum("srkgd,stkd->srkgt", query_rows, key_rows, preferred_element_type=jnp.float32)
        * 0.125
    )
    allowed = (query_pos[:, None] >= key_pos[None, :])[None, :, None, None, :]
    probs = jnp.where(allowed, jnp.exp(scores - log_total[..., None]), 0.0)
    back_values = jnp.einsum(
        "srkgt,srkgd->stkd",
        probs.astype(jnp.bfloat16),
        back_attend,
        preferred_element_type=jnp.float32,
    )
    back_probs = jnp.einsum(
        "srkgd,stkd->srkgt", back_attend, value_row_list, preferred_element_type=jnp.float32
    )
    back_scores = (probs * (back_probs - row_dot[..., None])).astype(jnp.bfloat16)
    back_queries = (
        jnp.einsum("srkgt,stkd->srkgd", back_scores, key_rows, preferred_element_type=jnp.float32)
        * 0.125
    )
    back_keys = (
        jnp.einsum("srkgt,srkgd->stkd", back_scores, query_rows, preferred_element_type=jnp.float32)
        * 0.125
    )
    return (back_queries, back_keys, back_values)


def forward_keys(state_now, query_rows, key_flat, value_flat, query_pos):
    seqs_here, rows_here = (key_flat.shape[0], key_flat.shape[1])
    key_heads, head_size = (query_rows.shape[2], query_rows.shape[4])
    current_size = block_size(rows_here)

    def forward_visit_block(block_index, state_in):
        first_key = block_index * current_size

        def forward_compute(state_arg):
            key_rows = lax.dynamic_slice_in_dim(
                key_flat, block_index * current_size, current_size, 1
            ).reshape(seqs_here, current_size, key_heads, head_size)
            value_row_list = lax.dynamic_slice_in_dim(
                value_flat, block_index * current_size, current_size, 1
            ).reshape(seqs_here, current_size, key_heads, head_size)
            key_pos = first_key + jnp.arange(current_size, dtype=jnp.int32)
            return attend_block(state_arg, query_rows, key_rows, value_row_list, query_pos, key_pos)

        return lax.cond(
            first_key <= query_pos[-1], forward_compute, lambda unchanged: unchanged, state_in
        )

    return lax.fori_loop(0, rows_here // current_size, forward_visit_block, state_now)


def backward_keys(
    state_now, query_rows, back_attend, log_total, row_dot, key_flat, value_flat, query_pos
):
    seqs_here, rows_here = (key_flat.shape[0], key_flat.shape[1])
    key_heads, head_size = (query_rows.shape[2], query_rows.shape[4])
    current_size = block_size(rows_here)

    def backward_visit_block(block_index, state_in):
        first_key = block_index * current_size

        def backward_compute(state_arg):
            back_queries, pair_terms = state_arg
            key_rows = lax.dynamic_slice_in_dim(
                key_flat, block_index * current_size, current_size, 1
            ).reshape(seqs_here, current_size, key_heads, head_size)
            value_row_list = lax.dynamic_slice_in_dim(
                value_flat, block_index * current_size, current_size, 1
            ).reshape(seqs_here, current_size, key_heads, head_size)
            key_pos = first_key + jnp.arange(current_size, dtype=jnp.int32)
            query_part, key_part, value_part = grad_block(
                query_rows,
                back_attend,
                log_total,
                row_dot,
                key_rows,
                value_row_list,
                query_pos,
                key_pos,
            )
            pair_part = jnp.concatenate(
                [
                    key_part.reshape(seqs_here, current_size, key_heads * head_size),
                    value_part.reshape(seqs_here, current_size, key_heads * head_size),
                ],
                axis=-1,
            )
            pair_slot = lax.dynamic_slice_in_dim(
                pair_terms, first_key, current_size, 0
            ) + jnp.transpose(pair_part, (1, 0, 2))
            pair_terms = lax.dynamic_update_slice_in_dim(pair_terms, pair_slot, first_key, 0)
            return (back_queries + query_part, pair_terms)

        return lax.cond(
            first_key <= query_pos[-1], backward_compute, lambda unchanged: unchanged, state_in
        )

    return lax.fori_loop(0, rows_here // current_size, backward_visit_block, state_now)


def body(
    inputs,
    query_weight,
    key_weight,
    value_matrix,
    out_weight,
    gate_weight,
    up_weight,
    down_weight,
    norm_gains,
    cotangent,
):
    seqs_here, rows_here, model_width = inputs.shape
    flat_rows = seqs_here * rows_here
    half_query, half_key, half_value, half_out, half_gate, half_up, half_down, half_gains = (
        lax.all_gather(query_weight, "dp", axis=1, tiled=True),
        lax.all_gather(key_weight, "dp", axis=1, tiled=True),
        lax.all_gather(value_matrix, "dp", axis=1, tiled=True),
        lax.all_gather(out_weight, "dp", axis=0, tiled=True),
        lax.all_gather(gate_weight, "dp", axis=1, tiled=True),
        lax.all_gather(up_weight, "dp", axis=1, tiled=True),
        lax.all_gather(down_weight, "dp", axis=0, tiled=True),
        lax.all_gather(norm_gains, "dp", axis=0, tiled=True),
    )
    (
        whole_query,
        whole_key,
        whole_value,
        whole_out,
        whole_gate,
        whole_up,
        whole_down,
        whole_gains,
    ) = (
        lax.all_gather(half_query, "ctx", axis=0, tiled=True),
        lax.all_gather(half_key, "ctx", axis=0, tiled=True),
        lax.all_gather(half_value, "ctx", axis=0, tiled=True),
        lax.all_gather(half_out, "ctx", axis=1, tiled=True),
        lax.all_gather(half_gate, "ctx", axis=0, tiled=True),
        lax.all_gather(half_up, "ctx", axis=0, tiled=True),
        lax.all_gather(half_down, "ctx", axis=1, tiled=True),
        lax.all_gather(half_gains, "ctx", axis=1, tiled=True),
    )
    gains = whole_gains.astype(jnp.float32)
    query_heads = whole_query.shape[1] // HEAD_WIDTH
    key_heads = whole_key.shape[1] // HEAD_WIDTH
    key_width = key_heads * HEAD_WIDTH
    group_size = query_heads // key_heads
    sequence_length = rows_here * lax.axis_size("ctx")
    query_pos = lax.axis_index("ctx") * rows_here + jnp.arange(rows_here, dtype=jnp.int32)
    cosine_table, sine_table = rope_tables(query_pos, HEAD_WIDTH // 2)
    tokens_wide = inputs.astype(jnp.float32).reshape(flat_rows, model_width)
    inv_first = lax.rsqrt(jnp.mean(tokens_wide * tokens_wide, axis=-1, keepdims=True) + EPSILON)
    unit_first = tokens_wide * inv_first
    normed = (unit_first * gains[0]).astype(jnp.bfloat16)
    query_linear = jnp.dot(normed, whole_query, preferred_element_type=jnp.float32)
    key_mapping = jnp.dot(normed, whole_key, preferred_element_type=jnp.float32)
    value_entries = jnp.dot(normed, whole_value, preferred_element_type=jnp.float32).astype(
        jnp.bfloat16
    )
    query_rows = apply_rotation(
        query_linear.reshape(seqs_here, rows_here, query_heads, HEAD_WIDTH),
        cosine_table,
        sine_table,
    ).astype(jnp.bfloat16)
    query_rows = query_rows.reshape(seqs_here, rows_here, key_heads, group_size, HEAD_WIDTH)
    rotated_keys = apply_rotation(
        key_mapping.reshape(seqs_here, rows_here, key_heads, HEAD_WIDTH), cosine_table, sine_table
    ).astype(jnp.bfloat16)
    rotated_keys = rotated_keys.reshape(seqs_here, rows_here, key_width)
    value_row_list = value_entries.reshape(seqs_here, rows_here, key_width)
    start_state = (
        jnp.full((seqs_here, rows_here, key_heads, group_size), MASKED_SCORE, jnp.float32),
        jnp.zeros((seqs_here, rows_here, key_heads, group_size), jnp.float32),
        jnp.zeros((seqs_here, rows_here, key_heads, group_size, HEAD_WIDTH), jnp.float32),
    )
    portion = (
        lax.all_gather(rotated_keys, "ctx", axis=1, tiled=True),
        lax.all_gather(value_row_list, "ctx", axis=1, tiled=True),
    )
    run_max, run_sum, weighted = forward_keys(
        start_state, query_rows, portion[0], portion[1], query_pos
    )
    log_total = run_max + jnp.log(run_sum)
    attended = (weighted / run_sum[..., None]).astype(jnp.bfloat16)
    attended_flat = attended.reshape(flat_rows, query_heads * HEAD_WIDTH)
    middle = tokens_wide + jnp.dot(attended_flat, whole_out, preferred_element_type=jnp.float32)
    inv_second = lax.rsqrt(jnp.mean(middle * middle, axis=-1, keepdims=True) + EPSILON)
    unit_second = middle * inv_second
    mixed_in = (unit_second * gains[1]).astype(jnp.bfloat16)
    gate_linear = jnp.dot(mixed_in, whole_gate, preferred_element_type=jnp.float32)
    lift_linear = jnp.dot(mixed_in, whole_up, preferred_element_type=jnp.float32)
    sigmoid_gate = jax.nn.sigmoid(gate_linear)
    hidden = (gate_linear * sigmoid_gate * lift_linear).astype(jnp.bfloat16)
    result = middle + jnp.dot(hidden, whole_down, preferred_element_type=jnp.float32)
    layer_out = result.astype(jnp.bfloat16).reshape(seqs_here, rows_here, model_width)
    back_out = cotangent.reshape(flat_rows, model_width)
    term_down = jnp.einsum("nf,nd->fd", hidden, back_out, preferred_element_type=jnp.float32)
    back_hidden = jnp.einsum("nd,fd->nf", back_out, whole_down, preferred_element_type=jnp.float32)
    back_gate = (
        back_hidden * lift_linear * sigmoid_gate * (1.0 + gate_linear * (1.0 - sigmoid_gate))
    ).astype(jnp.bfloat16)
    back_lift = (back_hidden * gate_linear * sigmoid_gate).astype(jnp.bfloat16)
    term_gate = jnp.einsum("nd,nf->df", mixed_in, back_gate, preferred_element_type=jnp.float32)
    term_lift = jnp.einsum("nd,nf->df", mixed_in, back_lift, preferred_element_type=jnp.float32)
    back_mixed = jnp.einsum(
        "nf,df->nd", back_gate, whole_gate, preferred_element_type=jnp.float32
    ) + jnp.einsum("nf,df->nd", back_lift, whole_up, preferred_element_type=jnp.float32)
    gain_second = jnp.sum(back_mixed * unit_second, axis=0)
    scaled_second = back_mixed * gains[1]
    back_middle = back_out.astype(jnp.float32) + inv_second * (
        scaled_second - unit_second * jnp.mean(scaled_second * unit_second, axis=-1, keepdims=True)
    )
    back_proj = back_middle.astype(jnp.bfloat16)
    term_out = jnp.einsum("na,nd->ad", attended_flat, back_proj, preferred_element_type=jnp.float32)
    back_attend = jnp.einsum(
        "nd,ad->na", back_proj, whole_out, preferred_element_type=jnp.float32
    ).astype(jnp.bfloat16)
    back_attend = back_attend.reshape(seqs_here, rows_here, key_heads, group_size, HEAD_WIDTH)
    row_dot = jnp.sum(back_attend.astype(jnp.float32) * attended.astype(jnp.float32), axis=-1)
    start_grads = (
        jnp.zeros((seqs_here, rows_here, key_heads, group_size, HEAD_WIDTH), jnp.float32),
        jnp.zeros((sequence_length, seqs_here, 2 * key_width), jnp.float32),
    )
    portion = (
        lax.all_gather(rotated_keys, "ctx", axis=1, tiled=True),
        lax.all_gather(value_row_list, "ctx", axis=1, tiled=True),
    )
    back_queries, pair_terms = backward_keys(
        start_grads, query_rows, back_attend, log_total, row_dot, portion[0], portion[1], query_pos
    )
    pair_sums = lax.psum_scatter(pair_terms, "ctx", scatter_dimension=0, tiled=True)
    pair_sums = jnp.transpose(pair_sums, (1, 0, 2))
    back_keys = pair_sums[..., :key_width]
    back_values = pair_sums[..., key_width:]
    query_back = unrotate(
        back_queries.reshape(seqs_here, rows_here, query_heads, HEAD_WIDTH),
        cosine_table,
        sine_table,
    )
    query_back = query_back.astype(jnp.bfloat16).reshape(flat_rows, query_heads * HEAD_WIDTH)
    key_back = unrotate(
        back_keys.reshape(seqs_here, rows_here, key_heads, HEAD_WIDTH), cosine_table, sine_table
    )
    key_back = key_back.astype(jnp.bfloat16).reshape(flat_rows, key_width)
    value_back = back_values.astype(jnp.bfloat16).reshape(flat_rows, key_width)
    term_query = jnp.einsum("nd,na->da", normed, query_back, preferred_element_type=jnp.float32)
    term_key = jnp.einsum("nd,na->da", normed, key_back, preferred_element_type=jnp.float32)
    term_value = jnp.einsum("nd,na->da", normed, value_back, preferred_element_type=jnp.float32)
    back_normed = (
        jnp.einsum("na,da->nd", query_back, whole_query, preferred_element_type=jnp.float32)
        + jnp.einsum("na,da->nd", key_back, whole_key, preferred_element_type=jnp.float32)
        + jnp.einsum("na,da->nd", value_back, whole_value, preferred_element_type=jnp.float32)
    )
    gain_first = jnp.sum(back_normed * unit_first, axis=0)
    scaled_first = back_normed * gains[0]
    input_grad = back_middle + inv_first * (
        scaled_first - unit_first * jnp.mean(scaled_first * unit_first, axis=-1, keepdims=True)
    )
    term_gains = jnp.stack([gain_first, gain_second])
    sum_query, sum_key, sum_value, sum_out, sum_gate, sum_lift, sum_down, sum_gains = (
        lax.psum_scatter(term_query, "ctx", scatter_dimension=0, tiled=True),
        lax.psum_scatter(term_key, "ctx", scatter_dimension=0, tiled=True),
        lax.psum_scatter(term_value, "ctx", scatter_dimension=0, tiled=True),
        lax.psum_scatter(term_out, "ctx", scatter_dimension=1, tiled=True),
        lax.psum_scatter(term_gate, "ctx", scatter_dimension=0, tiled=True),
        lax.psum_scatter(term_lift, "ctx", scatter_dimension=0, tiled=True),
        lax.psum_scatter(term_down, "ctx", scatter_dimension=1, tiled=True),
        lax.psum_scatter(term_gains, "ctx", scatter_dimension=1, tiled=True),
    )
    (
        final_query,
        final_key,
        final_value,
        final_out,
        final_gate,
        final_lift,
        final_down,
        final_gains,
    ) = (
        lax.psum_scatter(
            sum_query.astype(jnp.bfloat16), "dp", scatter_dimension=1, tiled=True
        ).astype(jnp.float32),
        lax.psum_scatter(
            sum_key.astype(jnp.bfloat16), "dp", scatter_dimension=1, tiled=True
        ).astype(jnp.float32),
        lax.psum_scatter(
            sum_value.astype(jnp.bfloat16), "dp", scatter_dimension=1, tiled=True
        ).astype(jnp.float32),
        lax.psum_scatter(
            sum_out.astype(jnp.bfloat16), "dp", scatter_dimension=0, tiled=True
        ).astype(jnp.float32),
        lax.psum_scatter(
            sum_gate.astype(jnp.bfloat16), "dp", scatter_dimension=1, tiled=True
        ).astype(jnp.float32),
        lax.psum_scatter(
            sum_lift.astype(jnp.bfloat16), "dp", scatter_dimension=1, tiled=True
        ).astype(jnp.float32),
        lax.psum_scatter(
            sum_down.astype(jnp.bfloat16), "dp", scatter_dimension=0, tiled=True
        ).astype(jnp.float32),
        lax.psum_scatter(
            sum_gains.astype(jnp.bfloat16), "dp", scatter_dimension=0, tiled=True
        ).astype(jnp.float32),
    )
    return (
        layer_out,
        input_grad.reshape(seqs_here, rows_here, model_width),
        final_query,
        final_key,
        final_value,
        final_out,
        final_gate,
        final_lift,
        final_down,
        final_gains,
    )


def solution(mesh):
    return jax.shard_map(
        body,
        mesh=mesh,
        in_specs=(
            P("dp", "ctx", None),
            P("ctx", "dp"),
            P("ctx", "dp"),
            P("ctx", "dp"),
            P("dp", "ctx"),
            P("ctx", "dp"),
            P("ctx", "dp"),
            P("dp", "ctx"),
            P("dp", "ctx"),
            P("dp", "ctx", None),
        ),
        out_specs=(
            P("dp", "ctx", None),
            P("dp", "ctx", None),
            P("ctx", "dp"),
            P("ctx", "dp"),
            P("ctx", "dp"),
            P("dp", "ctx"),
            P("ctx", "dp"),
            P("ctx", "dp"),
            P("dp", "ctx"),
            P("dp", "ctx"),
        ),
        check_vma=False,
    )
```

profile of v0, /device:TPU:0, one launch (start us, length us, event | category | flops | bytes accessed | tf_op | source)
XLA Modules:
  0.0 1184.2 jit_solution(4980652207166459051)
XLA Ops:
  7.3 6.2 all-gather.4
  25.6 25.2 %all-gather.3 = bf16[16,60,320]{2,1,0:T(8,128)(2,1)S(1)} all-gather(bf16[1,60,320]{2,1,0:T(8,128)(2,1)S(1)} %bitcast.362), channel_id=1, replica_groups=mesh['dp'=2,'ctx'=16] {'ctx'}, dimensions={0}, use_global_device_ids=true | all-gather | bytes 652800 | tf_op jit(solution)/shard_map/all_gather | solution.py:214
  55.7 17.0 %all-gather.1 = bf16[16,60,2]{1,2,0:T(2,128)(2,1)S(1)} all-gather(bf16[1,60,2]{1,2,0:T(2,128)(2,1)S(1)} %bitcast.385), channel_id=1, replica_groups=mesh['dp'=2,'ctx'=16] {'ctx'}, dimensions={0}, use_global_device_ids=true | all-gather | bytes 4080 | tf_op jit(solution)/shard_map/all_gather | solution.py:220
  79.3 22.8 %all-gather.7 = bf16[16,60,320]{2,1,0:T(8,128)(2,1)S(1)} all-gather(bf16[1,60,320]{2,1,0:T(8,128)(2,1)S(1)} %bitcast.363), channel_id=1, replica_groups=mesh['dp'=2,'ctx'=16] {'ctx'}, dimensions={0}, use_global_device_ids=true | all-gather | bytes 652800 | tf_op jit(solution)/shard_map/all_gather | solution.py:215
  105.7 7.2 all_gather.68
  113.0 6.4 all_gather.70
  119.6 6.1 all_gather.72
  138.0 13.0 %all-gather.21.cloned.1.call-done = bf16[2,2048,320]{1,2,0:T(8,128)(2,1)} async-done(((bf16[2,128,320]{1,2,0:T(8,128)(2,1)}), bf16[2,2048,320]{1,2,0:T(8,128)(2,1)}) %all-gather.21.cloned.1.call-update) | async-done | bytes 2621456 | tf_op jit(solution)/shard_map/all_gather | solution.py:256
  151.0 45.3 %all-gather.23.cloned.1.call-done = bf16[2,2048,320]{1,2,0:T(8,128)(2,1)} async-done(((bf16[2,128,320]{1,2,0:T(8,128)(2,1)}), bf16[2,2048,320]{1,2,0:T(8,128)(2,1)}) %all-gather.23.cloned.1.call-update) | async-done | bytes 2621456 | tf_op jit(solution)/shard_map/all_gather | solution.py:257
  197.3 14.3 %while.32 = (s32[]{:T(128)}, f32[2,128,5,3]{1,3,2,0:T(4,128)S(1)}, f32[2,128,5,3]{1,3,2,0:T(4,128)S(1)}, f32[2,128,5,3,64]{1,4,3,2,0:T(8,128)}, s32[128]{0:T(128...) while((s32[]{:T(128)}, f32[2,128,5,3]{1,3,2,0:T(4,128)S(1)}, ...), condition=%wide.region_6.7_spmd, body=%wide.region_1.6_spmd.sunk | while | flops 529440768 | bytes 30495556 | solution.py:127
  198.6 9.2 conditional.4
  216.2 36.8 %all-gather.29.cloned.1.call-done = bf16[16,60,2560]{2,1,0:T(8,128)(2,1)} async-done(((bf16[1,60,2560]{2,1,0:T(8,128)(2,1)}), bf16[16,60,2560]{2,1,0:T(8,128)(2,1)}) %all-gather.29.cloned.1.call-update) | async-done | bytes 4915216 | tf_op jit(solution)/shard_map/all_gather | solution.py:217
  253.0 7.3 reshape.347
  260.3 49.4 %all-gather.31.cloned.1.call-done = bf16[16,60,2560]{2,1,0:T(8,128)(2,1)} async-done(((bf16[1,60,2560]{2,1,0:T(8,128)(2,1)}), bf16[16,60,2560]{2,1,0:T(8,128)(2,1)}) %all-gather.31.cloned.1.call-update) | async-done | bytes 4915216 | tf_op jit(solution)/shard_map/all_gather | solution.py:218
  309.7 7.4 reshape.349
  326.1 40.5 %all-gather.33.cloned.1.call-done = bf16[16,60,2560]{2,1,0:T(8,128)(2,1)} async-done(((bf16[1,60,2560]{2,1,0:T(8,128)(2,1)}), bf16[16,60,2560]{2,1,0:T(8,128)(2,1)}) %all-gather.33.cloned.1.call-update) | async-done | bytes 4915216 | tf_op jit(solution)/shard_map/all_gather | solution.py:219
  366.6 7.5 reshape.351
  374.2 6.9 multiply_convert_fusion
  402.2 23.9 %while.33 = (s32[]{:T(128)}, f32[2,128,5,3,64]{1,4,3,2,0:T(8,128)S(1)}, f32[2048,2,640]{0,2,1:T(8,128)}, s32[128]{0:T(128)S(1)}, bf16[2,2048,320]{1,2,0:T(8,128)...) while((s32[]{:T(128)}, ...), condition=%wide.region_13.0_spmd, body=%wide.region_10.13_spmd.sunk | while | flops 1280147968 | bytes 117557200 | solution.py:176
  403.4 18.9 %conditional.5 = ((f32[2,128,5,3,64]{1,4,3,2,0:T(8,128)S(1)}, f32[2048,2,640]{0,2,1:T(8,128)})) conditional(s32[]{:T(128)} %convert_element_type.299, (f32[2,128,5,3,64]{1,4,3,2,0:T(8,128)S(1)}, f32[2048,2,640]{0,2,1:T(8,128)}) %tuple.104, (s32[]{:T(128)}, bf16[2,2048,320]{1,2,0:T(8,128)(2,1)}, s32[128]{0:T(128)S(1)}, s32[]{:T(128)}, ...), branch_computations={%region_11.11_spmd, %region_12.12_spmd} | conditional | flops 1280147968 | bytes 117556936 | solution.py:172
  448.1 152.3 %reduce-scatter.32.cloned.1.call-done = f32[128,2,640]{0,2,1:T(8,128)} async-done(((f32[2048,2,640]{0,2,1:T(8,128)}), f32[128,2,640]{0,2,1:T(8,128)}) %reduce-scatter.32.cloned.1.call-update) | async-done | bytes 655376 | tf_op jit(solution)/shard_map/reduce_scatter | solution.py:310
  605.4 416.3 %fusion.87 = (f32[64,960]{1,0:T(8,128)S(1)}, f32[64,320]{1,0:T(8,128)S(1)}, f32[64,320]{1,0:T(8,128)S(1)}, f32[960,64]{0,1:T(8,128)}, f32[64,2560]{1,0:T(8,128)}, /*index=5*/f32[64,2560]{1,0:T(8,128)}, f32[2560,64]{0,1:T(8,128)}) fusion(f32[960,960]{1,0:T(8,128)} %fusion.43, f32[960,320]{1,0:T(8,128)} %fusion.50, ...), kind=kCustom, calls=%all-reduce-scatter.7 | all-reduce-scatter fusion | flops 10485761 | bytes 41943552
  1021.7 34.5 %collective-permute-start.2 = (bf16[60,320]{1,0:T(8,128)(2,1)S(1)}, bf16[60,320]{1,0:T(8,128)(2,1)S(1)}, u32[]{:S(2)}, u32[]{:S(2)}) collective-permute-start(bf16[60,320]{1,0:T(8,128)(2,1)S(1)} %slice.79), channel_id=1, source_target_pairs={{0,1},{1,2},{2,3},{3,4},{4,5},{5,6},{6,7},{7,8},{8,9},{9,10},{10,1... | collective-permute-start | bytes 115208
  1120.3 30.0 %all-reduce.7 = bf16[2,960]{1,0:T(2,128)(2,1)S(1)} all-reduce(f32[2,960]{1,0:T(2,128)S(1)} %pad_maximum_fusion.2), channel_id=17, replica_groups=mesh['dp'=2,'ctx'=16] {'ctx'}, use_global_device_ids=true, to_apply=%region_32.33.clone | all-reduce | flops 1920 | bytes 11520
  (303 shorter events, 224.3 us)
Async XLA Ops:
  7.2 118.6 %all-gather.25.cloned.1.call-start = ((), (), s32[]{:S(2)}) async-start(), calls=%async_computation.14 | async-start | bytes 2228224 | tf_op jit(solution)/shard_map/all_gather | solution.py:213
  14.5 117.1 %all-gather.27.cloned.1.call-start = ((), (), s32[]{:S(2)}) async-start(), calls=%async_computation.15 | async-start | bytes 2228224 | tf_op jit(solution)/shard_map/all_gather | solution.py:216
  20.6 130.4 %all-gather.21.cloned.1.call-start = ((), (), s32[]{:S(2)}) async-start(), calls=%async_computation.8 | async-start | bytes 2785280 | tf_op jit(solution)/shard_map/all_gather | solution.py:256
  74.4 121.8 %all-gather.23.cloned.1.call-start = ((), (), s32[]{:S(2)}) async-start(), calls=%async_computation.9 | async-start | bytes 2785280 | tf_op jit(solution)/shard_map/all_gather | solution.py:257
  105.7 147.3 %all-gather.29.cloned.1.call-start = ((), (), s32[]{:S(2)}) async-start(), calls=%async_computation.16 | async-start | bytes 5570560 | tf_op jit(solution)/shard_map/all_gather | solution.py:217
  113.0 196.8 %all-gather.31.cloned.1.call-start = ((), (), s32[]{:S(2)}) async-start(), calls=%async_computation.17 | async-start | bytes 5570560 | tf_op jit(solution)/shard_map/all_gather | solution.py:218
  119.5 247.1 %all-gather.33.cloned.1.call-start = ((), (), s32[]{:S(2)}) async-start(), calls=%async_computation.18 | async-start | bytes 5570560 | tf_op jit(solution)/shard_map/all_gather | solution.py:219
  125.7 474.7 %reduce-scatter.32.cloned.1.call-start = ((), (), s32[]{:S(2)}) async-start(), calls=%async_computation.10 | async-start | bytes 11141120 | tf_op jit(solution)/shard_map/reduce_scatter | solution.py:310
  426.2 739.9 %reduce-scatter.42.cloned.1.call-start = ((), (), s32[]{:S(2)}) async-start(), calls=%async_computation.20 | async-start | bytes 122880
  605.4 455.2 %copy-start.47 = (u32[32]{0:T(128)S(1)}, u32[32]{0:T(128)}, u32[]{:S(2)}) copy-start(u32[32]{0:T(128)} %constant.95) | copy-start | bytes 388
  605.4 457.1 %copy-start.49 = (u32[32]{0:T(128)S(1)}, u32[32]{0:T(128)}, u32[]{:S(2)}) copy-start(u32[32]{0:T(128)} %constant.127) | copy-start | bytes 388
  1021.7 44.7 %collective-permute-start.2 = (bf16[60,320]{1,0:T(8,128)(2,1)S(1)}, bf16[60,320]{1,0:T(8,128)(2,1)S(1)}, u32[]{:S(2)}, u32[]{:S(2)}) collective-permute-start(bf16[60,320]{1,0:T(8,128)(2,1)S(1)} %slice.79), channel_id=1, source_target_pairs={{0,1},{1,2},{2,3},{3,4},{4,5},{5,6},{6,7},{7,8},{8,9},{9,10},{10,1... | collective-permute-start | bytes 115208
  1056.2 10.4 collective-permute-start.1
  1063.8 16.3 %collective-permute-start = (bf16[60,960]{1,0:T(8,128)(2,1)}, bf16[60,960]{1,0:T(8,128)(2,1)}, u32[]{:S(2)}, u32[]{:S(2)}) collective-permute-start(bf16[60,960]{1,0:T(8,128)(2,1)} %slice.77), channel_id=1, source_target_pairs={{0,1},{1,2},{2,3},{3,4},{4,5},{5,6},{6,7},{7,8},{8,9},{9,10},{10,1... | collective-permute-start | bytes 345608
  1067.8 99.9 %reduce-scatter.44.cloned.1.call-start = ((), (), s32[]{:S(2)}) async-start(), calls=%async_computation.21 | async-start | bytes 122880
  1074.0 22.5 %collective-permute-start.3 = (bf16[960,60]{0,1:T(8,128)(2,1)}, bf16[960,60]{0,1:T(8,128)(2,1)}, u32[]{:S(2)}, u32[]{:S(2)}) collective-permute-start(bf16[960,60]{0,1:T(8,128)(2,1)} %slice.80), channel_id=1, source_target_pairs={{0,1},{1,2},{2,3},{3,4},{4,5},{5,6},{6,7},{7,8},{8,9},{9,10},{10,1... | collective-permute-start | bytes 345608
  1076.7 22.8 %collective-permute-start.4 = (bf16[60,2560]{1,0:T(8,128)(2,1)}, bf16[60,2560]{1,0:T(8,128)(2,1)}, u32[]{:S(2)}, u32[]{:S(2)}) collective-permute-start(bf16[60,2560]{1,0:T(8,128)(2,1)} %slice.81), channel_id=1, source_target_pairs={{0,1},{1,2},{2,3},{3,4},{4,5},{5,6},{6,7},{7,8},{8,9},{9,10},{10,1... | collective-permute-start | bytes 921608
  1080.0 89.1 %reduce-scatter.40.cloned.1.call-start = ((), (), s32[]{:S(2)}) async-start(), calls=%async_computation.19 | async-start | bytes 368640
  1086.7 84.1 %reduce-scatter.46.cloned.1.call-start = ((), (), s32[]{:S(2)}) async-start(), calls=%async_computation.22 | async-start | bytes 368640
  1090.1 19.5 %collective-permute-start.5 = (bf16[60,2560]{1,0:T(8,128)(2,1)}, bf16[60,2560]{1,0:T(8,128)(2,1)}, u32[]{:S(2)}, u32[]{:S(2)}) collective-permute-start(bf16[60,2560]{1,0:T(8,128)(2,1)} %slice.82), channel_id=1, source_target_pairs={{0,1},{1,2},{2,3},{3,4},{4,5},{5,6},{6,7},{7,8},{8,9},{9,10},{10,1... | collective-permute-start | bytes 921608
  1094.5 60.9 %collective-permute-start.6 = (bf16[2560,60]{0,1:T(8,128)(2,1)S(1)}, bf16[2560,60]{0,1:T(8,128)(2,1)}, u32[]{:S(2)}, u32[]{:S(2)}) collective-permute-start(bf16[2560,60]{0,1:T(8,128)(2,1)S(1)} %slice.83), channel_id=1, source_target_pairs={{0,1},{1,2},{2,3},{3,4},{4,5},{5,6},{6,7},{7,8},{8,9},{9,10},{10,1... | collective-permute-start | bytes 921608
  1099.5 73.1 %reduce-scatter.34.cloned.1.call-start = ((), (), s32[]{:S(2)}) async-start(), calls=%async_computation.11 | async-start | bytes 491520 | tf_op jit(solution)/shard_map/reduce_scatter | solution.py:371
  1106.8 67.4 %reduce-scatter.36.cloned.1.call-start = ((), (), s32[]{:S(2)}) async-start(), calls=%async_computation.12 | async-start | bytes 491520 | tf_op jit(solution)/shard_map/reduce_scatter | solution.py:374
  1117.3 58.6 %reduce-scatter.38.cloned.1.call-start = ((), (), s32[]{:S(2)}) async-start(), calls=%async_computation.13 | async-start | bytes 491520 | tf_op jit(solution)/shard_map/reduce_scatter | solution.py:377
  (48 other events, 1487.4 us)
Sparse Core Ops, SparseCore 0:
  14.6 44.6 all-gather.24
  62.0 42.2 all-gather.26
  107.1 43.8 all-gather.20
  153.6 42.6 all-gather.22
  198.4 54.5 all-gather.28
  255.2 54.5 all-gather.30
  312.0 54.5 all-gather.32
  426.3 174.0 reduce-scatter.31
  1067.9 9.5 reduce-scatter.41
  1080.1 9.5 reduce-scatter.43
  1092.0 11.4 reduce-scatter.39
  1106.2 11.4 reduce-scatter.45
  1120.5 12.3 reduce-scatter.33
  1135.7 12.3 reduce-scatter.35
  1162.7 9.6 reduce-scatter.37
where the time goes:
time: 1190 us; the launch traced here: 1180 us
  blocking collectives  561 us (47%)
  waiting for transfers between devices  338 us (28%)
  local copies, waits for them, and re-layouts  101 us (8%)
  matrix products  86.3 us (7%)
  starting transfers between devices  53.6 us (5%)
  other arithmetic  23.3 us (2%)
  between operations  16.3 us (1%)
    unnamed x3, blocking collectives  451 us
    reduce_scatter x1, waiting for transfers between devices, body(): lax.psum_scatter(pair_terms, 'ctx', scatter_dimension=0, tiled=True)  152 us
    unnamed x130, local copies, waits for them, and re-layouts  67.9 us
    unnamed x11, starting transfers between devices  52.9 us
    all_gather x1, waiting for transfers between devices, body(): lax.all_gather(half_up, 'ctx', axis=0, tiled=True)  49.4 us
    all_gather x1, waiting for transfers between devices, body(): lax.all_gather(value_row_list, 'ctx', axis=1, tiled=True)  45.3 us
    all_gather x1, waiting for transfers between devices, body(): lax.all_gather(half_down, 'ctx', axis=1, tiled=True)  40.5 us
    all_gather x1, waiting for transfers between devices, body(): lax.all_gather(half_gate, 'ctx', axis=0, tiled=True)  36.8 us
  transfers between devices with their start and end apart: 22, of which 6 were waited for; matrix products, arithmetic and copies ran while one was open for 12% of the time, Pallas kernels for 0%

commit v1 on v0

v1 whole, which is shorter than its diff:
```python
import functools
import math

import jax
import jax.numpy as jnp
import numpy as np
from jax import lax
from jax.experimental import pallas as pl
from jax.experimental.pallas import tpu as pltpu
from jax.sharding import Mesh, PartitionSpec as P

HEAD = 64
EPSILON = 1e-05
MASKED = -1e30
FLOOR = -1e20
LOG2E = 1.4426950408889634
SCALE = 0.125 * LOG2E
BF = jnp.bfloat16
F32 = jnp.float32
SWAP = [(0, 1), (1, 0)]


def dot(a, b, ca, cb):
    return lax.dot_general(a, b, (((ca,), (cb,)), ((), ())), preferred_element_type=F32)


def rope_tables(positions, half):
    spectrum = jnp.exp(jnp.arange(half, dtype=F32) * (-math.log(100000.0) / half))
    angles = spectrum[:, None] * positions.astype(F32)[None, :]
    return jnp.cos(angles), jnp.sin(angles)


def rotate(vectors, cos, sin):
    rows = vectors.shape[-1]
    halves = vectors.reshape(-1, 2, HEAD // 2, rows)
    low, high = halves[:, 0], halves[:, 1]
    return jnp.stack([low * cos - high * sin, high * cos + low * sin], axis=1).reshape(-1, rows)


def allowed_mask(y, keys, rows):
    key_pos = lax.broadcasted_iota(jnp.int32, (keys, rows), 0) + y * keys
    row_pos = lax.broadcasted_iota(jnp.int32, (keys, rows), 1)
    return row_pos >= key_pos


def forward_kernel(line, group, place, q_ref, *refs):
    k_refs, v_refs = refs[:line], refs[line : 2 * line]
    o_ref, lse_ref, m_ref, l_ref, acc_ref = refs[2 * line :]
    z, y = place[0], place[1]
    keys, rows = k_refs[0].shape[1], q_ref.shape[1]
    for h in range(group):
        q = q_ref[h * HEAD : (h + 1) * HEAD, :]
        scores = dot(k_refs[0][...], q, 0, 0) * SCALE
        scores = jnp.where(allowed_mask(y, keys, rows), scores, MASKED)
        top = jnp.maximum(jnp.max(scores, axis=0, keepdims=True), FLOOR)
        probs = jnp.exp2(scores - top)
        m_ref[...] = top
        l_ref[...] = jnp.sum(probs, axis=0, keepdims=True)
        acc_ref[...] = dot(v_refs[0][...], probs.astype(BF), 1, 0)
        for s in range(1, line):

            @pl.when(s <= z)
            def _():
                scores = dot(k_refs[s][...], q, 0, 0) * SCALE
                old = m_ref[...]
                top = jnp.maximum(jnp.max(scores, axis=0, keepdims=True), old)
                probs = jnp.exp2(scores - top)
                shrink = jnp.exp2(old - top)
                m_ref[...] = top
                l_ref[...] = l_ref[...] * shrink + jnp.sum(probs, axis=0, keepdims=True)
                acc_ref[...] = acc_ref[...] * shrink + dot(v_refs[s][...], probs.astype(BF), 1, 0)

        total = l_ref[...]
        o_ref[h * HEAD : (h + 1) * HEAD, :] = acc_ref[...] / jnp.maximum(total, 1e-30)
        lse_ref[0, h : h + 1, :] = jnp.where(
            total > 0, m_ref[...] + jnp.log2(jnp.maximum(total, 1e-30)), MASKED
        )


def attend_forward(place, q, kvs, kv_heads):
    line = len(kvs)
    width, rows = q.shape
    group = width // HEAD // kv_heads
    keys = kvs[0].shape[1]
    k_specs = [pl.BlockSpec((HEAD, keys), lambda g: (g, 0))] * line
    v_specs = [pl.BlockSpec((HEAD, keys), lambda g: (g + kv_heads, 0))] * line
    pairs = width // HEAD * keys * line * rows
    return pl.pallas_call(
        functools.partial(forward_kernel, line, group),
        grid=(kv_heads,),
        in_specs=[
            pl.BlockSpec(memory_space=pltpu.SMEM),
            pl.BlockSpec((group * HEAD, rows), lambda g: (g, 0)),
            *k_specs,
            *v_specs,
        ],
        out_specs=[
            pl.BlockSpec((group * HEAD, rows), lambda g: (g, 0)),
            pl.BlockSpec((1, 8, rows), lambda g: (g, 0, 0)),
        ],
        out_shape=[
            jax.ShapeDtypeStruct((width, rows), F32),
            jax.ShapeDtypeStruct((kv_heads, 8, rows), F32),
        ],
        scratch_shapes=[
            pltpu.VMEM((1, rows), F32),
            pltpu.VMEM((1, rows), F32),
            pltpu.VMEM((HEAD, rows), F32),
        ],
        cost_estimate=pl.CostEstimate(
            flops=pairs * HEAD * 4, bytes_accessed=6 * width * rows, transcendentals=pairs
        ),
        compiler_params=pltpu.CompilerParams(vmem_limit_bytes=40 * 2**20),
        name="attend_forward",
    )(place, q, *kvs, *kvs)


def backward_kernel(
    step, group, has_more, place, q_ref, do_ref, lse_ref, dot_ref, k_ref, v_ref, *refs
):
    if has_more:
        more_k, more_v, dq_in, dq_ref, dk_ref, dv_ref = refs
    else:
        dq_ref, dk_ref, dv_ref = refs
    z, y = place[0], place[1]
    keys, rows = k_ref.shape[1], q_ref.shape[1]

    @pl.when(step <= z)
    def _():
        key, value = k_ref[...], v_ref[...]
        if has_more:
            dk, dv = more_k[...].astype(F32), more_v[...].astype(F32)
        else:
            dk = dv = jnp.zeros((HEAD, keys), F32)
        for h in range(group):
            at = slice(h * HEAD, (h + 1) * HEAD)
            q, do = q_ref[at, :], do_ref[at, :]
            scores = dot(key, q, 0, 0) * SCALE
            probs = jnp.exp2(scores - lse_ref[0, h : h + 1, :])
            if step == 0:
                probs = jnp.where(allowed_mask(y, keys, rows), probs, 0.0)
            back_probs = dot(value, do, 0, 0)
            back = (probs * (back_probs - dot_ref[0, h : h + 1, :])).astype(BF)
            dv = dv + dot(do, probs.astype(BF), 1, 1)
            dk = dk + dot(q, back, 1, 1) * 0.125
            dq = dot(key, back, 1, 0) * 0.125
            if has_more:
                dq = dq + dq_in[at, :]
            dq_ref[at, :] = dq
        dk_ref[...] = dk.astype(dk_ref.dtype)
        dv_ref[...] = dv.astype(dv_ref.dtype)

    @pl.when(step > z)
    def _():
        dq_ref[...] = jnp.zeros_like(dq_ref)
        dk_ref[...] = jnp.zeros_like(dk_ref)
        dv_ref[...] = jnp.zeros_like(dv_ref)


def attend_backward(place, step, q, do, lse, row_dot, kv, more, dq, kv_heads):
    width, rows = q.shape
    group = width // HEAD // kv_heads
    keys = kv.shape[1]
    has_more = more is not None
    wide = pl.BlockSpec((group * HEAD, rows), lambda g: (g, 0))
    stat = pl.BlockSpec((1, 8, rows), lambda g: (g, 0, 0))
    first = pl.BlockSpec((HEAD, keys), lambda g: (g, 0))
    second = pl.BlockSpec((HEAD, keys), lambda g: (g + kv_heads, 0))
    kind = F32 if step == 0 else BF
    pairs = width // HEAD * keys * rows
    return pl.pallas_call(
        functools.partial(backward_kernel, step, group, has_more),
        grid=(kv_heads,),
        in_specs=[pl.BlockSpec(memory_space=pltpu.SMEM), wide, wide, stat, stat, first, second]
        + ([first, second, wide] if has_more else []),
        out_specs=[wide, first, first],
        out_shape=[
            jax.ShapeDtypeStruct((width, rows), F32),
            jax.ShapeDtypeStruct((kv_heads * HEAD, keys), kind),
            jax.ShapeDtypeStruct((kv_heads * HEAD, keys), kind),
        ],
        cost_estimate=pl.CostEstimate(
            flops=pairs * HEAD * 10, bytes_accessed=12 * width * rows, transcendentals=pairs
        ),
        compiler_params=pltpu.CompilerParams(vmem_limit_bytes=40 * 2**20),
        name=f"attend_backward_{step}",
    )(place, q, do, lse, row_dot, kv, kv, *((more, more, dq) if has_more else ()))


def padded(count):
    return -(-count // 8) * 8


def pick(pair, index):
    return jnp.where(index == 0, pair[0], pair[1])


def body(
    inputs,
    query_weight,
    key_weight,
    value_matrix,
    out_weight,
    gate_weight,
    up_weight,
    down_weight,
    norm_gains,
    cotangent,
):
    seqs, part_rows, model = inputs.shape
    dps, line = lax.axis_size("dp"), lax.axis_size("z")
    ctx = line * 4
    z, y, c, d = (lax.axis_index(a) for a in ("z", "y", "c", "dp"))
    shard = model // ctx
    slot = padded(shard + 1)
    wide = slot * ctx
    rows = 2 * part_rows
    up_line = [(i, i + 1) for i in range(line - 1)]
    down_line = [(i + 1, i) for i in range(line - 1)]

    q_part, k_part = query_weight.shape[1], key_weight.shape[1]
    qkv_part = q_part + 2 * k_part
    half_ff = gate_weight.shape[1]
    kv_heads = k_part * dps // HEAD
    q_heads = q_part * dps // HEAD
    group = q_heads // kv_heads

    small = jnp.concatenate([query_weight, key_weight, value_matrix, out_weight.T], axis=1)
    gain_row = jnp.pad(norm_gains, ((0, slot - shard - 1), (0, small.shape[1] - shard)))
    small = jnp.concatenate([small, gain_row], axis=0)
    small = lax.all_gather(small, ("dp", "z", "y", "c"), axis=0, tiled=True)
    small = small.reshape(dps, wide, -1)
    large = jnp.concatenate([gate_weight, up_weight, down_weight.T], axis=1)
    large = jnp.pad(large, ((0, slot - shard), (0, 0)))
    large = lax.all_gather(large, ("z", "y", "c"), axis=0, tiled=True)
    w_gate, w_up, w_down = (large[:, i * half_ff : (i + 1) * half_ff] for i in range(3))

    both = jnp.stack([inputs, cotangent], axis=1)
    mine, theirs = pick((both[0], both[1]), c), pick((both[1], both[0]), c)
    theirs = lax.ppermute(theirs, "c", SWAP)
    first, second = pick((mine, theirs), c), pick((theirs, mine), c)
    both = jnp.concatenate([first, second], axis=1)
    spread_row = lax.broadcasted_iota(jnp.int32, (model, wide), 0)
    spread_col = lax.broadcasted_iota(jnp.int32, (model, wide), 1)
    spread = (
        (spread_row // shard == spread_col // slot) & (spread_row % shard == spread_col % slot)
    ).astype(BF)
    tokens = dot(both[0], spread, 1, 0)
    back_out = dot(both[1], spread, 1, 0)
    back_out_low = back_out.astype(BF)

    gains = small.reshape(dps, ctx, slot, -1)[:, :, shard, :shard]
    gains = jnp.pad(gains, ((0, 0), (0, 0), (0, slot - shard))).reshape(dps, wide).astype(F32)
    real = (jnp.arange(wide) % slot < shard)[None, :]

    inv_first = lax.rsqrt(jnp.sum(tokens * tokens, axis=-1, keepdims=True) / model + EPSILON)
    unit_first = tokens * inv_first
    normed = (unit_first * gains[0]).astype(BF)
    heads = [dot(small[i, :, :qkv_part], normed, 0, 1) for i in range(dps)]
    q_lin = jnp.concatenate([h[:q_part] for h in heads], axis=0)
    k_lin = jnp.concatenate([h[q_part : q_part + k_part] for h in heads], axis=0)
    v_lin = jnp.concatenate([h[q_part + k_part :] for h in heads], axis=0)
    positions = (2 * z + y) * rows + jnp.arange(rows, dtype=jnp.int32)
    cos, sin = rope_tables(positions, HEAD // 2)
    q = rotate(q_lin, cos, sin).astype(BF)
    kv = jnp.concatenate([rotate(k_lin, cos, sin).astype(BF), v_lin.astype(BF)], axis=0)

    kvs = [kv]
    for _ in range(line - 1):
        kvs.append(lax.ppermute(kvs[-1], "z", up_line))
    q_other = lax.ppermute(q, "y", SWAP)
    q_both = jnp.concatenate([pick((q, q_other), y), pick((q_other, q), y)], axis=1)
    place = jnp.stack([z, y]).astype(jnp.int32)
    o_both, lse_part = attend_forward(place, q_both, kvs, kv_heads)
    o_mine = pick((o_both[:, :rows], o_both[:, rows:]), y)
    o_send = pick((o_both[:, rows:], o_both[:, :rows]), y).astype(BF)
    o_other = lax.ppermute(o_send, "y", SWAP)
    lse_other = lax.ppermute(lse_part, "y", SWAP)
    top = jnp.maximum(lse_part, lse_other)
    lse = top + jnp.log2(jnp.exp2(lse_part - top) + jnp.exp2(lse_other - top))
    w_mine, w_other = (
        jnp.exp2(pick((s[..., :rows] - lse[..., :rows], s[..., rows:] - lse[..., rows:]), y))
        .at[:, :group]
        .get()
        .reshape(q_heads, 1, rows)
        for s in (lse_part, lse_other)
    )
    attended = (
        o_mine.reshape(q_heads, HEAD, rows) * w_mine
        + o_other.reshape(q_heads, HEAD, rows).astype(F32) * w_other
    )
    attended = attended.reshape(-1, rows).astype(BF)
    half_q = q_part
    proj = sum(
        dot(attended[i * half_q : (i + 1) * half_q], small[i, :, qkv_part:], 0, 1)
        for i in range(dps)
    )
    middle = tokens + jnp.where(real, proj, 0.0)
    inv_second = lax.rsqrt(jnp.sum(middle * middle, axis=-1, keepdims=True) / model + EPSILON)
    unit_second = middle * inv_second
    mixed_own = (unit_second * gains[1]).astype(BF)

    mixed_far = lax.ppermute(mixed_own, "dp", SWAP)
    back_far = lax.ppermute(back_out_low, "dp", SWAP)
    results = []
    for mixed, back in ((mixed_far, back_far), (mixed_own, back_out_low)):
        gate = dot(mixed, w_gate, 1, 0)
        lift = dot(mixed, w_up, 1, 0)
        sig = jax.nn.sigmoid(gate)
        hidden = (gate * sig * lift).astype(BF)
        back_hidden = dot(back, w_down, 1, 0)
        back_gate = (back_hidden * lift * sig * (1.0 + gate * (1.0 - sig))).astype(BF)
        back_lift = (back_hidden * gate * sig).astype(BF)
        partial = dot(hidden, w_down, 1, 1)
        back_mixed = dot(back_gate, w_gate, 1, 1) + dot(back_lift, w_up, 1, 1)
        results.append((hidden, back_gate, back_lift, partial, back_mixed))
    back_mixed = results[1][4] + lax.ppermute(results[0][4].astype(BF), "dp", SWAP).astype(F32)
    result = middle + results[1][3] + lax.ppermute(results[0][3].astype(BF), "dp", SWAP).astype(F32)
    layer_low = result.astype(BF)

    hidden, back_gate, back_lift = (
        jnp.concatenate([results[0][i], results[1][i]], axis=0) for i in range(3)
    )
    mixed = jnp.concatenate([mixed_far, mixed_own], axis=0)
    back = jnp.concatenate([back_far, back_out_low], axis=0)
    grads = jnp.concatenate(
        [
            dot(mixed, back_gate, 0, 0).astype(BF),
            dot(mixed, back_lift, 0, 0).astype(BF),
            dot(back, hidden, 0, 0).astype(BF),
        ],
        axis=1,
    )
    grads = lax.psum_scatter(grads, ("z", "y", "c"), scatter_dimension=0, tiled=True)

    gain_second = jnp.sum(back_mixed * unit_second, axis=0)
    scaled = back_mixed * gains[1]
    back_middle = back_out + inv_second * (
        scaled - unit_second * (jnp.sum(scaled * unit_second, axis=-1, keepdims=True) / model)
    )
    back_proj = back_middle.astype(BF)
    do = jnp.concatenate(
        [dot(small[i, :, qkv_part:], back_proj, 0, 1) for i in range(dps)], axis=0
    ).astype(BF)
    row_dot = jnp.sum(
        do.astype(F32).reshape(q_heads, HEAD, rows)
        * attended.astype(F32).reshape(q_heads, HEAD, rows),
        axis=1,
    )
    row_dot = jnp.pad(row_dot.reshape(kv_heads, group, rows), ((0, 0), (0, 8 - group), (0, 0)))
    do_other = lax.ppermute(do, "y", SWAP)
    dot_other = lax.ppermute(row_dot, "y", SWAP)
    do_both = jnp.concatenate([pick((do, do_other), y), pick((do_other, do), y)], axis=1)
    dot_both = jnp.concatenate(
        [pick((row_dot, dot_other), y), pick((dot_other, row_dot), y)], axis=2
    )
    more = dq = None
    for step in range(line - 1, -1, -1):
        dq, dk, dv = attend_backward(
            place, step, q_both, do_both, lse, dot_both, kvs[step], more, dq, kv_heads
        )
        if step:
            more = lax.ppermute(jnp.concatenate([dk, dv], axis=0), "z", down_line)
    dq_mine = pick((dq[:, :rows], dq[:, rows:]), y)
    dq_send = pick((dq[:, rows:], dq[:, :rows]), y).astype(BF)
    dq = dq_mine + lax.ppermute(dq_send, "y", SWAP).astype(F32)
    dq = rotate(dq, cos, -sin).astype(BF)
    dk = rotate(dk, cos, -sin).astype(BF)
    dv = dv.astype(BF)
    backs = [
        jnp.concatenate(
            [
                dq[i * q_part : (i + 1) * q_part],
                dk[i * k_part : (i + 1) * k_part],
                dv[i * k_part : (i + 1) * k_part],
            ],
            axis=0,
        )
        for i in range(dps)
    ]
    back_normed = sum(dot(backs[i], small[i, :, :qkv_part], 0, 1) for i in range(dps))
    gain_first = jnp.sum(back_normed * unit_first, axis=0)
    scaled = back_normed * gains[0]
    input_grad = back_middle + inv_first * (
        scaled - unit_first * (jnp.sum(scaled * unit_first, axis=-1, keepdims=True) / model)
    )

    terms = []
    for i in range(dps):
        term = jnp.concatenate(
            [
                dot(normed, backs[i], 0, 1).astype(BF),
                dot(back_proj, attended[i * half_q : (i + 1) * half_q], 0, 1).astype(BF),
            ],
            axis=1,
        )
        terms.append(term)
    small_grads = jnp.stack(terms).reshape(dps, line, 2, 2, slot, -1)
    gain_terms = jnp.stack([gain_first, gain_second]).reshape(dps, line, 2, 2, slot)
    gain_terms = gain_terms[..., :shard].astype(BF)
    small_grads = small_grads.at[:, :, :, :, shard, :shard].set(gain_terms)

    def fold(array, axis, name, index):
        parts = jnp.split(array, 2, axis=axis)
        keep = pick(parts, index).squeeze(axis)
        send = pick((parts[1], parts[0]), index).squeeze(axis)
        return (keep.astype(F32) + lax.ppermute(send, name, SWAP).astype(F32)).astype(BF)

    small_grads = fold(small_grads, 3, "c", c)
    columns = small_grads.shape[-1] // 2
    left, right = small_grads[..., :columns], small_grads[..., columns:]
    left = fold(fold(left, 0, "dp", d), 1, "y", y)
    right = fold(fold(right, 2, "y", y), 0, "dp", d)
    small_grads = jnp.concatenate([left, right], axis=-1)
    small_grads = lax.all_to_all(small_grads, "z", split_axis=0, concat_axis=0)
    small_grads = jnp.sum(small_grads.astype(F32), axis=0)
    final_gains = small_grads[shard : shard + 1, :shard]
    small_grads = small_grads[:shard]
    final_query = small_grads[:, :q_part]
    final_key = small_grads[:, q_part : q_part + k_part]
    final_value = small_grads[:, q_part + k_part : qkv_part]
    final_out = small_grads[:, qkv_part:].T

    grads = grads[:shard].astype(F32)
    final_gate, final_lift, final_down = (
        grads[:, i * half_ff : (i + 1) * half_ff] for i in range(3)
    )

    def give_back(array):
        mine, theirs = (
            pick((array[:part_rows], array[part_rows:]), c),
            pick((array[part_rows:], array[:part_rows]), c),
        )
        theirs = lax.ppermute(theirs, "c", SWAP)
        return jnp.stack([pick((mine, theirs), c), pick((theirs, mine), c)])

    layer_out = dot(layer_low, spread, 1, 1).astype(BF)
    input_grad = input_grad.reshape(rows, ctx, slot)[:, :, :shard].reshape(rows, model)
    return (
        give_back(layer_out),
        give_back(input_grad),
        final_query,
        final_key,
        final_value,
        final_out,
        final_gate,
        final_lift,
        final_down.T,
        final_gains,
    )


def solution(mesh):
    devices = mesh.devices
    dps, ctx = devices.shape
    inner = Mesh(devices.reshape(dps, ctx // 4, 2, 2), ("dp", "z", "y", "c"))
    along = ("z", "y", "c")
    rows, by_row, by_col = P("dp", along, None), P(along, "dp"), P("dp", along)
    return jax.shard_map(
        body,
        mesh=inner,
        in_specs=(
            rows, by_row, by_row, by_row, by_col, by_row, by_row, by_col, by_col, rows,
        ),
        out_specs=(
            rows, rows, by_row, by_row, by_row, by_col, by_row, by_row, by_col, by_col,
        ),
        check_vma=False,
    )
```

time: 1190 us -> 448 us (0.38)
  blocking collectives: 561 us -> 0 us
  waiting for transfers between devices: 338 us -> 231 us
  local copies, waits for them, and re-layouts: 101 us -> 26.8 us
  matrix products: 86.3 us -> 60.6 us
  other arithmetic: 23.3 us -> 46.3 us
  Pallas kernels: 0 us -> 18.8 us
    unnamed x3 -> x0, blocking collectives: 451 us -> none
    ppermute x0 -> x24, waiting for transfers between devices: none -> 155 us  [the longest x3 51.8 us: body(): more = lax.ppermute(jnp.concatenate([dk, dv], axis=0), 'z', down_line)]
    reduce_scatter x4 -> x1, waiting for transfers between devices: 152 us -> 0.01 us  [body(): lax.psum_scatter(grads, ('z', 'y', 'c'), scatter_dimension=0, tiled=True)]
    all_gather x7 -> x2, waiting for transfers between devices: 185 us -> 62.9 us  [the longest x1 62.9 us: body(): small = lax.all_gather(small, ('dp', 'z', 'y', 'c'), axis=0, tiled=True)]
    all_gather x11 -> x0, blocking collectives: 110 us -> none  [the longest x1 25.2 us: body(): lax.all_gather(half_key, 'ctx', axis=0, tiled=True)]
    unnamed x130 -> x123, local copies, waits for them, and re-layouts: 67.9 us -> 8.7 us
    unnamed x11 -> x0, starting transfers between devices: 52.9 us -> none
    ppermute x0 -> x24, starting transfers between devices: none -> 36.7 us  [the longest x3 14.8 us: body(): kvs.append(lax.ppermute(kvs[-1], 'z', up_line))]
  transfers between devices with their start and end apart: 22 -> 28, of which waited for: 6 -> 18; matrix products, arithmetic and copies ran while one was open for 12% -> 24% of each run, Pallas kernels for 0% -> 4%
where the time goes in v1:
time: 448 us; the launch traced here: 441 us
  waiting for transfers between devices  231 us (52%)
  matrix products  60.6 us (14%)
  other arithmetic  46.3 us (10%)
  starting transfers between devices  41.7 us (9%)
  local copies, waits for them, and re-layouts  26.8 us (6%)
  Pallas kernels  18.8 us (4%)
  between operations  15.7 us (4%)
    all_gather x1, waiting for transfers between devices, body(): small = lax.all_gather(small, ('dp', 'z', 'y', 'c'), axis=0, tiled=True)  62.9 us
    dot_general x29, matrix products, dot(): lax.dot_general(a, b, (((ca,), (cb,)), ((), ())), preferred_element_type=...  60.6 us
    ppermute x3, waiting for transfers between devices, body(): more = lax.ppermute(jnp.concatenate([dk, dv], axis=0), 'z', down_line)  51.8 us
    ppermute x3, waiting for transfers between devices, body(): kvs.append(lax.ppermute(kvs[-1], 'z', up_line))  29.7 us
    ppermute x5, waiting for transfers between devices, fold(): lax.ppermute(send, name, SWAP).astype(F32)  20.3 us
    ppermute x1, waiting for transfers between devices, body(): dq = dq_mine + lax.ppermute(dq_send, 'y', SWAP).astype(F32)  17 us
    ppermute x3, starting transfers between devices, body(): kvs.append(lax.ppermute(kvs[-1], 'z', up_line))  14.8 us
    ppermute x1, waiting for transfers between devices, body(): lax.ppermute(results[0][3].astype(BF), 'dp', SWAP).astype(F32)  13.6 us
  transfers between devices with their start and end apart: 28, of which 18 were waited for; matrix products, arithmetic and copies ran while one was open for 24% of the time, Pallas kernels for 4%

profile of v1, /device:TPU:0, one launch (start us, length us, event | category | flops | bytes accessed | tf_op | source)
XLA Modules:
  0.0 440.5 jit_solution(4983277007377156675)
XLA Ops:
  16.5 62.9 %all-gather.3.cloned.1.call-done = bf16[2048,1280]{1,0:T(8,128)(2,1)} async-done(((bf16[64,1280]{1,0:T(8,128)(2,1)}), bf16[2048,1280]{1,0:T(8,128)(2,1)}) %all-gather.3.cloned.1.call-update) | async-done | bytes 5242896 | tf_op jit(solution)/shard_map/all_gather | solution.py:231
  90.5 12.5 %collective-permute-done.2.refs_1_.refs_5_.k_ref.v_ref = bf16[640,256]{1,0:T(8,128)(2,1)S(1)} collective-permute-done((bf16[640,256]{1,0:T(8,128)(2,1)S(1)}, bf16[640,256]{1,0:T(8,128)(2,1)S(1)}, u32[]{:S(2)}, u32[]{:S(2)}) %collective-permute-start.2) | collective-permute-done | bytes 327712 | tf_op jit(solution)/shard_map/ppermute | solution.py:270
  103.0 6.6 %collective-permute-start.3 = (bf16[640,256]{1,0:T(8,128)(2,1)S(1)}, bf16[640,256]{1,0:T(8,128)(2,1)S(1)}, u32[]{:S(2)}, u32[]{:S(2)}) collective-permute-start(bf16[640,256]{1,0:T(8,128)(2,1)S(1)} %collective-permute-done.2.refs_1_.refs_5_.k_ref.v_ref), channel_id=1, source_target_pairs={{0,4},{4,8},{8,12},{1,5},{5,9},{9,13},{2,6},{6,10},{10,14},{3,7},{... | collective-permute-start | bytes 983048 | tf_op jit(solution)/shard_map/ppermute | solution.py:270
  114.5 4.3 collective-permute-done.3.refs_2_.refs_6_.k_ref.v_ref
  118.8 4.4 collective-permute-start.4
  124.4 12.9 %collective-permute-done.4.refs_3_.refs_7_.k_ref.v_ref = bf16[640,256]{1,0:T(8,128)(2,1)S(1)} collective-permute-done((bf16[640,256]{1,0:T(8,128)(2,1)S(1)}, bf16[640,256]{1,0:T(8,128)(2,1)S(1)}, u32[]{:S(2)}, u32[]{:S(2)}) %collective-permute-start.4) | collective-permute-done | bytes 327712 | tf_op jit(solution)/shard_map/ppermute | solution.py:270
  139.3 8.5 %attend_forward.1 = (f32[960,512]{1,0:T(8,128)S(1)}, f32[5,8,512]{2,1,0:T(8,128)S(1)}) custom-call(s32[2]{0:T(128)S(1)} %pad_add_fusion.place, bf16[960,512]{1,0:T(8,128)(2,1)S(1)} %pad_maximum_fusion.6.q_ref, bf16[640,256]{1,0:T(8,128)(2,1)S(1)} %pad_maximum_fusion.20.refs_0_.refs_4_.k_ref.v_ref, bf16[640,256]{1,0:T(8,128)(2,1)S(1)} %copy-done.5, ...), custom_call_target="tpu_custom_call" | custom-call | flops 2013265920 | bytes 2949120 | tf_op jit(solution)/shard_map/attend_forward/pallas_call | solution.py:88
  153.4 7.0 %collective-permute-done.6 = bf16[960,256]{1,0:T(8,128)(2,1)} collective-permute-done((bf16[960,256]{1,0:T(8,128)(2,1)}, bf16[960,256]{1,0:T(8,128)(2,1)}, u32[]{:S(2)}, u32[]{:S(2)}) %collective-permute-start.6) | collective-permute-done | bytes 491552 | tf_op jit(solution)/shard_map/ppermute | solution.py:277
  170.9 6.3 %collective-permute-done.7 = bf16[256,1024]{1,0:T(8,128)(2,1)} collective-permute-done((bf16[256,1024]{1,0:T(8,128)(2,1)S(1)}, bf16[256,1024]{1,0:T(8,128)(2,1)}, u32[]{:S(2)}, u32[]{:S(2)}) %collective-permute-start.7) | collective-permute-done | bytes 524320 | tf_op jit(solution)/shard_map/ppermute | solution.py:303
  208.1 4.2 collective-permute-done.13
  220.4 8.8 %collective-permute-done.14.refs_0_.refs_1_ = bf16[640,256]{1,0:T(8,128)(2,1)S(1)} collective-permute-done((bf16[640,256]{1,0:T(8,128)(2,1)S(1)}, bf16[640,256]{1,0:T(8,128)(2,1)S(1)}, u32[]{:S(2)}, u32[]{:S(2)}) %collective-permute-start.14) | collective-permute-done | bytes 327712 | tf_op jit(solution)/shard_map/ppermute | solution.py:363
  237.1 12.5 %collective-permute-done.15.refs_0_.refs_1_ = bf16[640,256]{1,0:T(8,128)(2,1)S(1)} collective-permute-done((bf16[640,256]{1,0:T(8,128)(2,1)}, bf16[640,256]{1,0:T(8,128)(2,1)S(1)}, u32[]{:S(2)}, u32[]{:S(2)}) %collective-permute-start.15) | collective-permute-done | bytes 327712 | tf_op jit(solution)/shard_map/ppermute | solution.py:363
  259.2 30.5 %collective-permute-done.16.refs_0_.refs_1_ = bf16[640,256]{1,0:T(8,128)(2,1)S(1)} collective-permute-done((bf16[640,256]{1,0:T(8,128)(2,1)}, bf16[640,256]{1,0:T(8,128)(2,1)S(1)}, u32[]{:S(2)}, u32[]{:S(2)}) %collective-permute-start.16) | collective-permute-done | bytes 327712 | tf_op jit(solution)/shard_map/ppermute | solution.py:363
  291.3 7.7 %attend_backward_0.1 = (f32[960,512]{1,0:T(8,128)S(1)}, f32[320,256]{1,0:T(8,128)S(1)}, f32[320,256]{1,0:T(8,128)S(1)}) custom-call(s32[2]{0:T(128)S(1)} %pad_add_fusion.place, bf16[960,512]{1,0:T(8,128)(2,1)S(1)} %pad_maximum_fusion.6.q_ref, bf16[960,512]{1,0:T(8,128)(2,1)S(1)} %pad_maximum_fusion.7.do_ref, f32[5,8,512]{2,1,0:T(8,128)S(1)} %multiply_add_fusion.2.lse_ref, ...), custom_call_target="tpu_custom_call" | custom-call | flops 1258291200 | bytes 5898240 | tf_op jit(solution)/shard_map/attend_backward_0/pallas_call | solution.py:171
  301.3 17.0 %collective-permute-done.17 = bf16[960,256]{1,0:T(8,128)(2,1)S(1)} collective-permute-done((bf16[960,256]{1,0:T(8,128)(2,1)S(1)}, bf16[960,256]{1,0:T(8,128)(2,1)S(1)}, u32[]{:S(2)}, u32[]{:S(2)}) %collective-permute-start.17) | collective-permute-done | bytes 491552 | tf_op jit(solution)/shard_map/ppermute | solution.py:366
  328.2 4.5 %copy.51 = bf16[1024,1280]{1,0:T(8,128)(2,1)} copy(bf16[1024,1280]{0,1:T(8,128)(2,1)} %pad_maximum_fusion.2) | data formatting | bytes 5242880 | tf_op jit(solution)/shard_map/concatenate | solution.py:390
  338.6 4.6 %pad_maximum_fusion.1 = bf16[2,4,2,2,64,1280]{5,4,3,2,1,0:T(8,128)(2,1)} fusion(bf16[1,4,2,2,64,1280]{5,4,3,2,1,0:T(8,128)(2,1)S(1)} %bitcast.162, bf16[1,4,2,2,64,1280]{5,4,3,2,1,0:T(8,128)(2,1)} %bitcast.163), kind=kLoop, calls=%fused_computation.1 | loop fusion | flops 2621440 | bytes 10485760 | tf_op jit(solution)/shard_map/stack | solution.py:398
  345.4 4.4 select_bitcast_fusion
  354.1 13.6 %collective-permute-done.8 = bf16[256,1024]{1,0:T(8,128)(2,1)S(1)} collective-permute-done((bf16[256,1024]{1,0:T(8,128)(2,1)}, bf16[256,1024]{1,0:T(8,128)(2,1)S(1)}, u32[]{:S(2)}, u32[]{:S(2)}) %collective-permute-start.8) | collective-permute-done | bytes 524320 | tf_op jit(solution)/shard_map/ppermute | solution.py:318
  372.0 4.6 %fusion = bf16[2,4,2,64,1280]{4,3,2,1,0:T(8,128)(2,1)S(1)} fusion(bf16[2,4,2,64,1280]{4,3,2,1,0:T(8,128)(2,1)} %collective-permute-done.19, pred[]{:T(512)S(6)} %eq.23, bf16[2,4,2,2,64,1280]{5,4,3,2,1,0:T(8,128)(2,1)} %scatter.4), kind=kLoop, calls=%fused_computation.3 | loop fusion | flops 6553600 | bytes 10485761 | tf_op jit(solution)/shard_map/convert_element_type | solution.py:407
  379.6 14.3 %collective-permute-done.22 = bf16[2,4,64,640]{3,2,1,0:T(8,128)(2,1)S(1)} collective-permute-done((bf16[2,4,64,640]{3,2,1,0:T(8,128)(2,1)S(1)}, bf16[2,4,64,640]{3,2,1,0:T(8,128)(2,1)S(1)}, u32[]{:S(2)}, u32[]{:S(2)}) %collective-permute-start.22) | collective-permute-done | bytes 655392 | tf_op jit(solution)/shard_map/ppermute | solution.py:407
  399.2 5.5 %collective-permute-done.23 = bf16[4,64,640]{2,1,0:T(8,128)(2,1)} collective-permute-done((bf16[4,64,640]{2,1,0:T(8,128)(2,1)}, bf16[4,64,640]{2,1,0:T(8,128)(2,1)}, u32[]{:S(2)}, u32[]{:S(2)}) %collective-permute-start.23) | collective-permute-done | bytes 327712 | tf_op jit(solution)/shard_map/ppermute | solution.py:407
  408.2 4.9 %all-to-all-start = ((bf16[4,64,1280]{2,1,0:T(8,128)(2,1)}), bf16[4,64,1280]{2,1,0:T(8,128)(2,1)S(1)}, u32[]{:S(2)}, u32[]{:S(2)}) async-start(bf16[4,64,1280]{2,1,0:T(8,128)(2,1)} %pad_maximum_fusion.11), calls=%async_computation | async-start | bytes 1310720 | tf_op jit(solution)/shard_map/all_to_all | solution.py:415
  416.3 13.0 %all-to-all-done = bf16[4,64,1280]{2,1,0:T(8,128)(2,1)S(1)} async-done(((bf16[4,64,1280]{2,1,0:T(8,128)(2,1)}), bf16[4,64,1280]{2,1,0:T(8,128)(2,1)S(1)}, u32[]{:S(2)}, u32[]{:S(2)}) %all-to-all-start) | async-done | bytes 655392 | tf_op jit(solution)/shard_map/all_to_all | solution.py:415
  (306 shorter events, 149.5 us)
Async XLA Ops:
  7.2 72.3 %all-gather.3.cloned.1.call-start = ((), (), s32[]{:S(2)}) async-start(), calls=%async_computation.2 | async-start | bytes 5406720 | tf_op jit(solution)/shard_map/all_gather | solution.py:231
  9.7 158.3 %all-gather.5.cloned.1.call-start = ((), (), s32[]{:S(2)}) async-start(), calls=%async_computation.3 | async-start | bytes 8355840 | tf_op jit(solution)/shard_map/all_gather | solution.py:235
  11.7 419.7 %reduce-scatter.2.cloned.1.call-start = ((), (), s32[]{:S(2)}) async-start(), calls=%async_computation.4 | async-start | bytes 8355840 | tf_op jit(solution)/shard_map/reduce_scatter | solution.py:334
  84.8 18.2 %collective-permute-start.2 = (bf16[640,256]{1,0:T(8,128)(2,1)S(1)}, bf16[640,256]{1,0:T(8,128)(2,1)S(1)}, u32[]{:S(2)}, u32[]{:S(2)}) collective-permute-start(bf16[640,256]{1,0:T(8,128)(2,1)S(1)} %pad_maximum_fusion.20.refs_0_.refs_4_.k_ref.v_ref), channel_id=1, source_target_pairs={{0,4},{4,8},{8,12},{1,5},{5,9},{9,13},{2,6},{6,10},{10,14},{3,7},{... | collective-permute-start | bytes 983048 | tf_op jit(solution)/shard_map/ppermute | solution.py:270
  88.9 34.3 %collective-permute-start.1 = (bf16[960,256]{1,0:T(8,128)(2,1)S(1)}, bf16[960,256]{1,0:T(8,128)(2,1)}, u32[]{:S(2)}, u32[]{:S(2)}) collective-permute-start(bf16[960,256]{1,0:T(8,128)(2,1)S(1)} %bitcast.168), channel_id=1, source_target_pairs={{0,2},{2,0},{1,3},{3,1},{4,6},{6,4},{5,7},{7,5},{8,10},{10,8},{9,1... | collective-permute-start | bytes 1474568 | tf_op jit(solution)/shard_map/ppermute | solution.py:271
  103.0 15.8 %collective-permute-start.3 = (bf16[640,256]{1,0:T(8,128)(2,1)S(1)}, bf16[640,256]{1,0:T(8,128)(2,1)S(1)}, u32[]{:S(2)}, u32[]{:S(2)}) collective-permute-start(bf16[640,256]{1,0:T(8,128)(2,1)S(1)} %collective-permute-done.2.refs_1_.refs_5_.k_ref.v_ref), channel_id=1, source_target_pairs={{0,4},{4,8},{8,12},{1,5},{5,9},{9,13},{2,6},{6,10},{10,14},{3,7},{... | collective-permute-start | bytes 983048 | tf_op jit(solution)/shard_map/ppermute | solution.py:270
  113.1 54.9 %collective-permute-start.10 = (bf16[256,1024]{1,0:T(8,128)(2,1)}, bf16[256,1024]{1,0:T(8,128)(2,1)}, u32[]{:S(2)}, u32[]{:S(2)}) collective-permute-start(bf16[256,1024]{1,0:T(8,128)(2,1)} %get-tuple-element.118), channel_id=1, source_target_pairs={{0,16},{16,0},{1,17},{17,1},{2,18},{18,2},{3,19},{19,3},{4,20},{20... | collective-permute-start | bytes 1572872 | tf_op jit(solution)/shard_map/ppermute | solution.py:304
  118.8 18.5 %collective-permute-start.4 = (bf16[640,256]{1,0:T(8,128)(2,1)S(1)}, bf16[640,256]{1,0:T(8,128)(2,1)S(1)}, u32[]{:S(2)}, u32[]{:S(2)}) collective-permute-start(bf16[640,256]{1,0:T(8,128)(2,1)S(1)} %collective-permute-done.3.refs_2_.refs_6_.k_ref.v_ref), channel_id=1, source_target_pairs={{0,4},{4,8},{8,12},{1,5},{5,9},{9,13},{2,6},{6,10},{10,14},{3,7},{... | collective-permute-start | bytes 983048 | tf_op jit(solution)/shard_map/ppermute | solution.py:270
  149.7 10.7 %collective-permute-start.6 = (bf16[960,256]{1,0:T(8,128)(2,1)}, bf16[960,256]{1,0:T(8,128)(2,1)}, u32[]{:S(2)}, u32[]{:S(2)}) collective-permute-start(bf16[960,256]{1,0:T(8,128)(2,1)} %select_convert_fusion.1), channel_id=1, source_target_pairs={{0,2},{2,0},{1,3},{3,1},{4,6},{6,4},{5,7},{7,5},{8,10},{10,8},{9,1... | collective-permute-start | bytes 1474568 | tf_op jit(solution)/shard_map/ppermute | solution.py:277
  166.2 11.0 %collective-permute-start.7 = (bf16[256,1024]{1,0:T(8,128)(2,1)S(1)}, bf16[256,1024]{1,0:T(8,128)(2,1)}, u32[]{:S(2)}, u32[]{:S(2)}) collective-permute-start(bf16[256,1024]{1,0:T(8,128)(2,1)S(1)} %multiply_convert_fusion.6), channel_id=1, source_target_pairs={{0,16},{16,0},{1,17},{17,1},{2,18},{18,2},{3,19},{19,3},{4,20},{20... | collective-permute-start | bytes 1572872 | tf_op jit(solution)/shard_map/ppermute | solution.py:303
  185.0 10.0 %collective-permute-start.11 = (bf16[256,1024]{1,0:T(8,128)(2,1)S(1)}, bf16[256,1024]{1,0:T(8,128)(2,1)S(1)}, u32[]{:S(2)}, u32[]{:S(2)}) collective-permute-start(bf16[256,1024]{1,0:T(8,128)(2,1)S(1)} %fusion.56), channel_id=1, source_target_pairs={{0,16},{16,0},{1,17},{17,1},{2,18},{18,2},{3,19},{19,3},{4,20},{20... | collective-permute-start | bytes 1572872 | tf_op jit(solution)/shard_map/ppermute | solution.py:317
  202.0 10.3 %collective-permute-start.12 = (bf16[960,256]{1,0:T(8,128)(2,1)S(1)}, bf16[960,256]{1,0:T(8,128)(2,1)S(1)}, u32[]{:S(2)}, u32[]{:S(2)}) collective-permute-start(bf16[960,256]{1,0:T(8,128)(2,1)S(1)} %get-tuple-element.55), channel_id=1, source_target_pairs={{0,2},{2,0},{1,3},{3,1},{4,6},{6,4},{5,7},{7,5},{8,10},{10,8},{9,1... | collective-permute-start | bytes 1474568 | tf_op jit(solution)/shard_map/ppermute | solution.py:351
  213.5 15.8 %collective-permute-start.14 = (bf16[640,256]{1,0:T(8,128)(2,1)S(1)}, bf16[640,256]{1,0:T(8,128)(2,1)S(1)}, u32[]{:S(2)}, u32[]{:S(2)}) collective-permute-start(bf16[640,256]{1,0:T(8,128)(2,1)S(1)} %pad_maximum_fusion.21), channel_id=1, source_target_pairs={{4,0},{8,4},{12,8},{5,1},{9,5},{13,9},{6,2},{10,6},{14,10},{7,3},{... | collective-permute-start | bytes 983048 | tf_op jit(solution)/shard_map/ppermute | solution.py:363
  232.2 17.4 %collective-permute-start.15 = (bf16[640,256]{1,0:T(8,128)(2,1)}, bf16[640,256]{1,0:T(8,128)(2,1)S(1)}, u32[]{:S(2)}, u32[]{:S(2)}) collective-permute-start(bf16[640,256]{1,0:T(8,128)(2,1)} %pad_maximum_fusion.22), channel_id=1, source_target_pairs={{4,0},{8,4},{12,8},{5,1},{9,5},{13,9},{6,2},{10,6},{14,10},{7,3},{... | collective-permute-start | bytes 983048 | tf_op jit(solution)/shard_map/ppermute | solution.py:363
  254.0 35.7 %collective-permute-start.16 = (bf16[640,256]{1,0:T(8,128)(2,1)}, bf16[640,256]{1,0:T(8,128)(2,1)S(1)}, u32[]{:S(2)}, u32[]{:S(2)}) collective-permute-start(bf16[640,256]{1,0:T(8,128)(2,1)} %pad_maximum_fusion.23), channel_id=1, source_target_pairs={{4,0},{8,4},{12,8},{5,1},{9,5},{13,9},{6,2},{10,6},{14,10},{7,3},{... | collective-permute-start | bytes 983048 | tf_op jit(solution)/shard_map/ppermute | solution.py:363
  299.1 19.2 %collective-permute-start.17 = (bf16[960,256]{1,0:T(8,128)(2,1)S(1)}, bf16[960,256]{1,0:T(8,128)(2,1)S(1)}, u32[]{:S(2)}, u32[]{:S(2)}) collective-permute-start(bf16[960,256]{1,0:T(8,128)(2,1)S(1)} %select_convert_fusion), channel_id=1, source_target_pairs={{0,2},{2,0},{1,3},{3,1},{4,6},{6,4},{5,7},{7,5},{8,10},{10,8},{9,1... | collective-permute-start | bytes 1474568 | tf_op jit(solution)/shard_map/ppermute | solution.py:366
  349.7 22.3 %collective-permute-start.19 = (bf16[2,4,2,64,1280]{4,3,2,1,0:T(8,128)(2,1)}, bf16[2,4,2,64,1280]{4,3,2,1,0:T(8,128)(2,1)}, u32[]{:S(2)}, u32[]{:S(2)}) collective-permute-start(bf16[2,4,2,64,1280]{4,3,2,1,0:T(8,128)(2,1)} %select_bitcast_fusion), channel_id=1, source_target_pairs={{0,1},{1,0},{2,3},{3,2},{4,5},{5,4},{6,7},{7,6},{8,9},{9,8},{10,11... | collective-permute-start | bytes 7864328 | tf_op jit(solution)/shard_map/ppermute | solution.py:407
  353.3 14.4 %collective-permute-start.8 = (bf16[256,1024]{1,0:T(8,128)(2,1)}, bf16[256,1024]{1,0:T(8,128)(2,1)S(1)}, u32[]{:S(2)}, u32[]{:S(2)}) collective-permute-start(bf16[256,1024]{1,0:T(8,128)(2,1)} %fusion.53), channel_id=1, source_target_pairs={{0,16},{16,0},{1,17},{17,1},{2,18},{18,2},{3,19},{19,3},{4,20},{20... | collective-permute-start | bytes 1572872 | tf_op jit(solution)/shard_map/ppermute | solution.py:318
  372.0 41.3 %collective-permute-start.9 = (bf16[128,960]{0,1:T(8,128)(2,1)}, bf16[128,960]{0,1:T(8,128)(2,1)}, u32[]{:S(2)}, u32[]{:S(2)}) collective-permute-start(bf16[128,960]{0,1:T(8,128)(2,1)} %broadcast_select_fusion.6), channel_id=1, source_target_pairs={{0,1},{1,0},{2,3},{3,2},{4,5},{5,4},{6,7},{7,6},{8,9},{9,8},{10,11... | collective-permute-start | bytes 737288 | tf_op jit(solution)/shard_map/ppermute | solution.py:434
  376.7 17.2 %collective-permute-start.22 = (bf16[2,4,64,640]{3,2,1,0:T(8,128)(2,1)S(1)}, bf16[2,4,64,640]{3,2,1,0:T(8,128)(2,1)S(1)}, u32[]{:S(2)}, u32[]{:S(2)}) collective-permute-start(bf16[2,4,64,640]{3,2,1,0:T(8,128)(2,1)S(1)} %select_bitcast_fusion.1), channel_id=1, source_target_pairs={{0,2},{2,0},{1,3},{3,1},{4,6},{6,4},{5,7},{7,5},{8,10},{10,8},{9,1... | collective-permute-start | bytes 1966088 | tf_op jit(solution)/shard_map/ppermute | solution.py:407
  378.0 17.8 %collective-permute-start.20 = (bf16[4,2,64,640]{3,2,0,1:T(8,128)(2,1)S(1)}, bf16[4,2,64,640]{3,2,0,1:T(8,128)(2,1)S(1)}, u32[]{:S(2)}, u32[]{:S(2)}) collective-permute-start(bf16[4,2,64,640]{3,2,0,1:T(8,128)(2,1)S(1)} %select_bitcast_fusion.2), channel_id=1, source_target_pairs={{0,16},{16,0},{1,17},{17,1},{2,18},{18,2},{3,19},{19,3},{4,20},{20... | collective-permute-start | bytes 1966088 | tf_op jit(solution)/shard_map/ppermute | solution.py:407
  395.0 9.7 %collective-permute-start.23 = (bf16[4,64,640]{2,1,0:T(8,128)(2,1)}, bf16[4,64,640]{2,1,0:T(8,128)(2,1)}, u32[]{:S(2)}, u32[]{:S(2)}) collective-permute-start(bf16[4,64,640]{2,1,0:T(8,128)(2,1)} %select_bitcast_fusion.5), channel_id=1, source_target_pairs={{0,16},{16,0},{1,17},{17,1},{2,18},{18,2},{3,19},{19,3},{4,20},{20... | collective-permute-start | bytes 983048 | tf_op jit(solution)/shard_map/ppermute | solution.py:407
  396.8 9.4 %collective-permute-start.21 = (bf16[4,64,640]{2,1,0:T(8,128)(2,1)}, bf16[4,64,640]{2,1,0:T(8,128)(2,1)}, u32[]{:S(2)}, u32[]{:S(2)}) collective-permute-start(bf16[4,64,640]{2,1,0:T(8,128)(2,1)} %select_bitcast_fusion.6), channel_id=1, source_target_pairs={{0,2},{2,0},{1,3},{3,1},{4,6},{6,4},{5,7},{7,5},{8,10},{10,8},{9,1... | collective-permute-start | bytes 983048 | tf_op jit(solution)/shard_map/ppermute | solution.py:407
  408.2 21.1 %all-to-all-start = ((bf16[4,64,1280]{2,1,0:T(8,128)(2,1)}), bf16[4,64,1280]{2,1,0:T(8,128)(2,1)S(1)}, u32[]{:S(2)}, u32[]{:S(2)}) async-start(bf16[4,64,1280]{2,1,0:T(8,128)(2,1)} %pad_maximum_fusion.11), calls=%async_computation | async-start | bytes 1310720 | tf_op jit(solution)/shard_map/all_to_all | solution.py:415
  (66 other events, 671.0 us)
Sparse Core Ops, SparseCore 0:
  11.4 67.9 all-gather.2
  81.7 79.7 all-gather.4
  237.2 131.6 reduce-scatter.1
